TPU v7x, 32 devices: a whole 2x2x4 slice. The times are simulated.
32 devices in a mesh: groups: 2 (over y), dp: 16 (over z, x, core).
Axes of the slice: x: 2, y: 2, z: 4, core: 2. Of those that a mesh axis runs over, the one named last changes fastest.
Arguments:
- query_states: bfloat16 [128, 128, 2048], P(('groups', 'dp')), parts along dimension 0, may hold values from -4.5 to 4.5
- key_states: bfloat16 [128, 128, 512], P(('groups', 'dp')), parts along dimension 0, may hold values from -4.5 to 4.5
- value_states: bfloat16 [128, 128, 512], P(('groups', 'dp')), parts along dimension 0, may hold values from -56 to 56
- out_weight: bfloat16 [2048, 2048], P('dp'), may hold values from -0.125 to 0.125
- token_ids: int32 [128, 128], P(('groups', 'dp')), parts along dimension 0, may hold values from 0 to 31999, as said below
- keep_flags: int32 [128], P(('groups', 'dp')), parts along dimension 0, may hold values from 0 to 1, as said below
- list_ids: int32 [128, 128], P(('groups', 'dp')), parts along dimension 0, may hold values from 0 to 1023, as said below
- owner_map: int32 [2048], P('groups'), parts along dimension 0, may hold values from 0 to 15, as said below
Outputs:
- doc_vectors: bfloat16 [96, 2048], P(('groups', 'dp')), parts along dimension 0
- token_vectors: bfloat16 [16384, 2048], P(('groups', 'dp')), parts along dimension 0
- token_keys: int32 [16384], P(('groups', 'dp')), parts along dimension 0
There are 2 independent parts, one for each index of `groups`. A program takes and returns all parts, laid end to end along the dimension named above; an argument that names none is the same for every part. Nothing has to cross between parts.
Inputs may be any that keep to these rules, and one draw needn't show every extreme that they name: `token_ids`: in each document the ids are 0 exactly from its length on, and its length lies between 96 and 128. `keep_flags`: exactly 48 documents have the flag 1. `list_ids`: the tokens of the 4 documents of one index of dp name lists of any one owner between 16 and 48 times, exactly 48 times for some owner; over all 64 documents the lists of each owner are named exactly 512 times. `owner_map`: every owner holds exactly 64 lists.
All inputs are finite; a program needn't handle non-finite values.
Results may differ from a plain program's by a relative error of at most 0.0057.
Values may be sent and summed in bfloat16 or wider, within the bound.
A program may use at most 64 MiB of HBM per device.

v0:
```python
import math
import jax
import jax.numpy as jnp
from jax import lax
from jax.sharding import PartitionSpec as P

HEAD_DIM = 128


def carried_in(part, axis, combine, identity):
    place = lax.axis_index(axis)
    gathered = lax.all_gather(part, axis)
    state = jnp.zeros_like(part) + jnp.asarray(identity, part.dtype)

    def one(lap, state):
        return combine(state, lax.dynamic_index_in_dim(gathered, lap, 0, False))

    return lax.fori_loop(0, place, one, state)


def add_counts(earlier, later):
    return earlier + later


def normalize(values):
    return (values * lax.rsqrt(jnp.mean(values * values, axis=-1, keepdims=True) + 1e-06)).astype(
        jnp.bfloat16
    )


def attend(query_states, key_states, value_states, token_ids):
    doc_count, length, features = query_states.shape
    kv_features = key_states.shape[2]
    kv_count = kv_features // HEAD_DIM
    group_size = features // kv_features
    queries = query_states.reshape(doc_count, length, kv_count, group_size, HEAD_DIM)
    keys_split = key_states.reshape(doc_count, length, kv_count, HEAD_DIM)
    values_split = value_states.reshape(doc_count, length, kv_count, HEAD_DIM)
    scores = jnp.einsum(
        "nqhgd,nshd->nhgqs", queries, keys_split, preferred_element_type=jnp.float32
    ) / math.sqrt(HEAD_DIM)
    present = token_ids != 0
    scores = jnp.where(present[:, None, None, None, :], scores, -jnp.inf)
    row_max = jnp.max(scores, axis=-1, keepdims=True)
    weights = jnp.exp(scores - row_max)
    weights = (weights / jnp.sum(weights, axis=-1, keepdims=True)).astype(jnp.bfloat16)
    attended = jnp.einsum(
        "nhgqs,nshd->nqhgd", weights, values_split, preferred_element_type=jnp.float32
    )
    attended = attended.reshape(doc_count, length, features).astype(jnp.bfloat16)
    counts = jnp.sum(present.astype(jnp.float32), axis=1)
    pooled_attended = (
        jnp.einsum(
            "nt,ntf->nf", present.astype(jnp.bfloat16), attended, preferred_element_type=jnp.float32
        )
        / counts[:, None]
    )
    return (attended, pooled_attended)


def project(rows, pooled_attended, out_weight):
    piece = lax.all_gather(out_weight, "dp", axis=0, tiled=True)
    row_sum = jnp.dot(rows, piece, preferred_element_type=jnp.float32)
    pooled_sum = jnp.dot(
        pooled_attended, piece.astype(jnp.float32), precision=lax.Precision.HIGHEST
    )
    return (row_sum, pooled_sum)


def send_to_owners(rows, usable, sort_keys, owners, axis_size):
    row_count, width = rows.shape
    capacity = 3 * row_count // (2 * axis_size)
    owner_index = jnp.arange(axis_size, dtype=jnp.int32)
    member = ((owners[:, None] == owner_index[None, :]) & usable[:, None]).astype(jnp.int32)
    running = jnp.cumsum(member, axis=0)
    within = jnp.take_along_axis(running, owners[:, None], axis=1)[:, 0] - 1
    slots = jnp.where(usable, owners * capacity + within, axis_size * capacity)
    packed = jnp.zeros((axis_size * capacity, width), rows.dtype).at[slots].set(rows, mode="drop")
    packed_keys = (
        jnp.full((axis_size * capacity,), -1, jnp.int32).at[slots].set(sort_keys, mode="drop")
    )
    arrived, arrived_keys = (
        lax.all_to_all(
            packed.reshape(axis_size, capacity, width),
            "dp",
            split_axis=0,
            concat_axis=0,
            tiled=True,
        ),
        lax.all_to_all(
            packed_keys.reshape(axis_size, capacity), "dp", split_axis=0, concat_axis=0, tiled=True
        ),
    )
    arrived = arrived.reshape(-1, width)
    arrived_keys = arrived_keys.reshape(-1)
    filled = arrived_keys >= 0
    smaller = jnp.sum(filled[None, :] & (arrived_keys[None, :] < arrived_keys[:, None]), axis=1)
    targets = jnp.where(filled, smaller, row_count)
    sorted_rows = jnp.zeros((row_count, width), rows.dtype).at[targets].set(arrived, mode="drop")
    sorted_keys = jnp.full((row_count,), -1, jnp.int32).at[targets].set(arrived_keys, mode="drop")
    return (sorted_rows, sorted_keys)


def shards(
    query_states, key_states, value_states, out_weight, token_ids, keep_flags, list_ids, owner_map
):
    axis_size = lax.axis_size("dp")
    my_index = lax.axis_index("dp")
    slot_count = keep_flags.shape[0]
    kept_slots = 3 * slot_count // 4
    before = carried_in(keep_flags, "dp", add_counts, jnp.zeros_like(keep_flags))
    totals = lax.psum(keep_flags.astype(jnp.float32), "dp").astype(jnp.int32)
    earlier = jnp.cumsum(totals) - totals
    occupied = keep_flags == 1
    position = (earlier + before).astype(jnp.int32)
    doc_rank = jnp.where(occupied, position, -1)
    attended, pooled_attended = attend(query_states, key_states, value_states, token_ids)
    doc_count, length, features = attended.shape
    flat_rows = attended.reshape(doc_count * length, features)
    owners = jnp.take(owner_map, list_ids, axis=0).reshape(-1)
    usable_grid = occupied[:, None] & (token_ids != 0)
    positions = jnp.arange(length, dtype=jnp.int32)
    sort_keys = jnp.where(usable_grid, doc_rank[:, None] * length + positions[None, :], -1).reshape(
        -1
    )
    usable = usable_grid.reshape(-1)
    projected, pooled = project(flat_rows, pooled_attended, out_weight)
    unit_tokens = normalize(projected)
    token_vectors, token_keys = send_to_owners(unit_tokens, usable, sort_keys, owners, axis_size)
    unit_docs = normalize(pooled)
    every_doc, every_rank = (
        lax.all_gather(unit_docs, "dp", axis=0, tiled=True),
        lax.all_gather(doc_rank, "dp", axis=0, tiled=True),
    )
    wanted = jnp.arange(kept_slots, dtype=jnp.int32) * axis_size + my_index
    picker = (every_rank[None, :] == wanted[:, None]).astype(jnp.bfloat16)
    doc_vectors = jnp.dot(picker, every_doc, preferred_element_type=jnp.float32).astype(
        jnp.bfloat16
    )
    return (doc_vectors, token_vectors, token_keys)


def solution(mesh):
    return jax.shard_map(
        shards,
        mesh=mesh,
        in_specs=(
            P(("groups", "dp"), None, None),
            P(("groups", "dp"), None, None),
            P(("groups", "dp"), None, None),
            P("dp", None),
            P(("groups", "dp"), None),
            P(("groups", "dp")),
            P(("groups", "dp"), None),
            P("groups"),
        ),
        out_specs=(P(("groups", "dp"), None), P(("groups", "dp"), None), P(("groups", "dp"))),
        check_vma=False,
    )
```

profile of v0, /device:TPU:0, one launch (start us, length us, event | category | flops | bytes accessed | tf_op | source)
XLA Modules:
  0.0 237.1 jit_solution(729401904148163551)
XLA Ops:
  7.2 0.7 all-gather.4.cloned.1.call-update
  8.6 35.5 %psum.7 = f32[4]{0:T(128)S(1)} all-reduce(f32[4]{0:T(128)S(1)} %convert_element_type.46), channel_id=1, replica_groups=mesh['groups'=2,'dp'=16] {'dp'}, use_global_device_ids=true, to_apply=%region_0.1 | all-reduce | flops 4 | bytes 32 | tf_op jit(solution)/shard_map/psum | solution.py:112
  44.1 1.2 dynamic-slice
  46.0 0.9 dynamic-update-slice
  46.9 8.3 %all-reduce = s32[64]{0:T(128)S(1)} all-reduce(s32[64]{0:T(128)S(1)} %dynamic-update-slice), channel_id=2, replica_groups=mesh['groups'=2,'dp'=16] {'dp'}, use_global_device_ids=true, to_apply=%add | all-reduce | flops 64 | bytes 512
  55.4 0.7 fusion.35
  56.1 2.3 gather_fusion
  58.4 0.7 broadcast_compare_fusion.2
  59.8 0.8 select_bitcast_fusion
  60.5 0.7 bitcast_select_fusion.1
  61.2 1.2 reduce-window.20
  62.8 4.5 %gather_fusion.1 = s32[512]{0:T(512)S(1)} fusion(s32[512,16]{0,1:T(8,128)S(1)} %bitcast_bitcast_fusion, s32[512]{0:T(512)S(1)} %bitcast.79), kind=kCustom, calls=%fused_computation.1 | custom fusion | bytes 8192 | tf_op jit(solution)/shard_map/jit(take_along_axis)/gather | solution.py:76
  67.3 2.4 %scatter_custom_fusion = s32[768]{0:T(1024)S(1)} fusion(s32[512]{0:T(512)S(1)} %bitcast.89, s32[512]{0:T(512)S(1)} %get-tuple-element.35, s32[]{:T(128)} %constant.29.clone.1), kind=kCustom, calls=%fused_computation.67 | custom fusion | bytes 3076 | tf_op jit(solution)/shard_map/scatter | solution.py:80
  69.8 0.7 all_to_all.9
  70.5 6.3 %all-to-all-start = ((s32[16,1,48]{2,1,0:T(1,128)}), s32[16,1,48]{2,1,0:T(1,128)S(1)}, u32[]{:S(2)}, u32[]{:S(2)}) async-start(s32[16,1,48]{2,1,0:T(1,128)} %all_to_all.9), calls=%async_computation | async-start | bytes 16384 | tf_op jit(solution)/shard_map/all_to_all | solution.py:90
  76.8 1.0 copy.40
  77.8 3.3 %reshape.386 = bf16[4,128,4,4,128]{4,3,2,1,0:T(4,128)(2,1)S(1)} reshape(bf16[4,128,2048]{2,1,0:T(8,128)(2,1)} %param.10) | data formatting | bytes 4194304 | tf_op jit(solution)/shard_map/reshape | solution.py:36
  81.2 0.7 fusion.6
  82.0 1.7 fusion.45
  83.7 0.7 fusion.13
  84.4 2.9 %copy.32 = bf16[4,128,4,4,128]{4,3,2,1,0:T(4,128)(2,1)} copy(bf16[4,128,4,4,128]{1,4,3,2,0:T(8,128)(2,1)S(1)} %bitcast.80) | data formatting | bytes 4194304 | tf_op jit(solution)/shard_map/convert_element_type | solution.py:50
  87.3 4.5 %convert_element_type.57 = bf16[512,2048]{1,0:T(8,128)(2,1)} reshape(bf16[4,128,4,4,128]{4,3,2,1,0:T(4,128)(2,1)} %copy.32) | data formatting | bytes 4194304 | tf_op jit(solution)/shard_map/convert_element_type | solution.py:50
  91.8 10.5 %multiply_reduce_fusion = (f32[512]{0:T(512)S(1)}, f32[512,2048]{1,0:T(8,128)}) fusion(bf16[512,2048]{1,0:T(8,128)(2,1)} %convert_element_type.57, bf16[2048,2048]{1,0:T(8,128)(2,1)} %all-gather.4.cloned.1.call-done), kind=kOutput, calls=%fused_computation.13 | convolution fusion | flops 4297063936 | bytes 14682112 | tf_op jit(solution)/shard_map/dot_general | solution.py:63
  102.3 7.4 %scatter_custom_fusion.1 = bf16[768,2048]{1,0:T(8,128)(2,1)} fusion(s32[512]{0:T(512)S(1)} %bitcast.90, f32[512,2048]{1,0:T(8,128)} %get-tuple-element.45, f32[512]{0:T(512)S(1)} %add_rsqrt_fusion, bf16[]{:T(256)} %constant.40.clone.1), kind=kCustom, calls=%fused_computation.18 | custom fusion | flops 2097152 | bytes 7342082 | tf_op jit(solution)/shard_map/scatter | solution.py:78
  109.7 6.0 %all-to-all-start.1 = ((bf16[16,48,2048]{2,1,0:T(8,128)(2,1)}), bf16[16,48,2048]{2,1,0:T(8,128)(2,1)}, u32[]{:S(2)}, u32[]{:S(2)}) async-start(bf16[16,48,2048]{2,1,0:T(8,128)(2,1)} %bitcast.24), calls=%async_computation.1 | async-start | bytes 6291456 | tf_op jit(solution)/shard_map/all_to_all | solution.py:83
  115.9 71.5 %all-reduce.1 = s32[64]{0:T(128)S(1)} all-reduce(s32[64]{0:T(128)S(1)} %dynamic-update-slice.1), channel_id=1, replica_groups=mesh['groups'=2,'dp'=16] {'dp'}, use_global_device_ids=true, to_apply=%add.1 | all-reduce | flops 64 | bytes 512
  188.8 0.7 reduce.9
  190.1 3.9 %scatter_custom_fusion.3 = s32[512]{0:T(512)} fusion(s32[768]{0:T(1024)S(1)} %fusion.28, s32[768]{0:T(1024)S(1)} %reshape.438, s32[]{:T(128)} %constant.29.clone.1), kind=kCustom, calls=%fused_computation.72 | custom fusion | bytes 2052 | tf_op jit(solution)/shard_map/scatter | solution.py:100
  194.0 5.9 %multiply_reduce_fusion.1 = (f32[4]{0:T(128)S(1)}, f32[4,2048]{1,0:T(4,128)S(1)}) fusion(bf16[2048,2048]{1,0:T(8,128)(2,1)} %all-gather.4.cloned.1.call-done, f32[4,1,2048]{2,1,0:T(1,128)S(1)} %fusion.26, f32[4]{0:T(128)S(1)} %convert_reduce_fusion.1), kind=kOutput, calls=%fused_computation.40 | convolution fusion | flops 201351168 | bytes 8454176 | tf_op jit(solution)/shard_map/dot_general | solution.py:64
  200.0 20.1 %all-gather.1 = bf16[16,4,2048]{2,1,0:T(4,128)(2,1)S(1)} all-gather(bf16[1,4,2048]{2,1,0:T(4,128)(2,1)S(1)} %fusion.24), channel_id=1, replica_groups=mesh['groups'=2,'dp'=16] {'dp'}, dimensions={0}, use_global_device_ids=true | all-gather | bytes 278528 | tf_op jit(solution)/shard_map/all_gather | solution.py:132
  220.1 0.8 convolution_convert_fusion
  220.9 9.3 %scatter_custom_fusion.2 = bf16[512,2048]{1,0:T(8,128)(2,1)} fusion(s32[768]{0:T(1024)S(1)} %fusion.28, bf16[768,2048]{1,0:T(8,128)(2,1)} %bitcast.25, bf16[]{:T(256)} %constant.40.clone.1), kind=kCustom, calls=%fused_computation.28 | custom fusion | bytes 2097664 | tf_op jit(solution)/shard_map/scatter | solution.py:99
  (48 shorter events, 4.6 us)
Async XLA Ops:
  7.2 49.0 %copy-start = (s32[1024]{0:T(1024)S(1)}, s32[1024]{0:T(1024)}, u32[]{:S(2)}) copy-start(s32[1024]{0:T(1024)} %param.17) | copy-start | bytes 12292
  7.2 69.6 %copy-start.1 = (bf16[4,128,512]{2,1,0:T(8,128)(2,1)S(1)}, bf16[4,128,512]{2,1,0:T(8,128)(2,1)}, u32[]{:S(2)}) copy-start(bf16[4,128,512]{2,1,0:T(8,128)(2,1)} %param.12) | copy-start | bytes 1572868
  7.2 84.6 %all-gather.4.cloned.1.call-start = ((), (), s32[]{:S(2)}) async-start(), calls=%async_computation.2 | async-start | bytes 8912896 | tf_op jit(solution)/shard_map/all_gather | solution.py:62
  67.3 13.8 %copy-start.2 = (bf16[4,128,512]{2,1,0:T(8,128)(2,1)S(1)}, bf16[4,128,512]{2,1,0:T(8,128)(2,1)}, u32[]{:S(2)}) copy-start(bf16[4,128,512]{2,1,0:T(8,128)(2,1)} %param.11) | copy-start | bytes 1572868
  70.5 39.2 %all-to-all-start = ((s32[16,1,48]{2,1,0:T(1,128)}), s32[16,1,48]{2,1,0:T(1,128)S(1)}, u32[]{:S(2)}, u32[]{:S(2)}) async-start(s32[16,1,48]{2,1,0:T(1,128)} %all_to_all.9), calls=%async_computation | async-start | bytes 16384 | tf_op jit(solution)/shard_map/all_to_all | solution.py:90
  82.0 1.7 copy-start.3
  109.7 111.2 %all-to-all-start.1 = ((bf16[16,48,2048]{2,1,0:T(8,128)(2,1)}), bf16[16,48,2048]{2,1,0:T(8,128)(2,1)}, u32[]{:S(2)}, u32[]{:S(2)}) async-start(bf16[16,48,2048]{2,1,0:T(8,128)(2,1)} %bitcast.24), calls=%async_computation.1 | async-start | bytes 6291456 | tf_op jit(solution)/shard_map/all_to_all | solution.py:83
Sparse Core Ops, SparseCore 0:
  10.2 78.0 all-gather.3
where the time goes:
time: 238 us; the launch traced here: 237 us
  blocking collectives  135 us (57%)
  local copies, waits for them, and re-layouts  38.4 us (16%)
  matrix products  19.2 us (8%)
  other arithmetic  16.1 us (7%)
  between operations  14.9 us (6%)
  starting transfers between devices  12.3 us (5%)
    unnamed x2, blocking collectives  79.8 us
    psum x1, blocking collectives, shards(): totals = lax.psum(keep_flags.astype(jnp.float32), 'dp').astype(jnp.int32)  35.5 us
    all_gather x1, blocking collectives, shards(): lax.all_gather(unit_docs, 'dp', axis=0, tiled=True)  20.1 us
    dot_general x1, matrix products, project(): row_sum = jnp.dot(rows, piece, preferred_element_type=jnp.float32)  10.5 us
    scatter x1, local copies, waits for them, and re-layouts, send_to_owners(): jnp.zeros((row_count, width), rows.dtype).at[targets]  9.31 us
    convert_element_type x2, local copies, waits for them, and re-layouts, attend(): attended.reshape(doc_count, length, features).astype(jnp.bfloat16)  7.39 us
    scatter x1, other arithmetic, send_to_owners(): jnp.zeros((axis_size * capacity, width), rows.dtype).at[slots]  7.38 us
    all_to_all x1, starting transfers between devices, send_to_owners(): lax.all_to_all(packed_keys.reshape(axis_size, capacity), 'dp', split_axis...  6.32 us
  transfers between devices with their start and end apart: 3, of which 0 were waited for; matrix products, arithmetic and copies ran while one was open for 27% of the time, Pallas kernels for 0%

commit v1 on v0

--- a/solution.py
+++ b/solution.py
@@ -5,6 +5,18 @@
 from jax.sharding import PartitionSpec as P
 
 HEAD_DIM = 128
+
+
+def collect(x, axis, dim):
+    ways, here = (lax.axis_size(axis), lax.axis_index(axis))
+    grown, reach = (x, 1)
+    while reach < ways:
+        theirs = lax.ppermute(grown, axis, [(d, d ^ reach) for d in range(ways)])
+        mine_first = jnp.concatenate([grown, theirs], axis=dim)
+        theirs_first = jnp.concatenate([theirs, grown], axis=dim)
+        grown = jnp.where(here & reach == 0, mine_first, theirs_first)
+        reach = 2 * reach
+    return grown
 
 
 def carried_in(part, axis, combine, identity):
@@ -129,7 +141,7 @@
     token_vectors, token_keys = send_to_owners(unit_tokens, usable, sort_keys, owners, axis_size)
     unit_docs = normalize(pooled)
     every_doc, every_rank = (
-        lax.all_gather(unit_docs, "dp", axis=0, tiled=True),
+        collect(unit_docs, "dp", 0),
         lax.all_gather(doc_rank, "dp", axis=0, tiled=True),
     )
     wanted = jnp.arange(kept_slots, dtype=jnp.int32) * axis_size + my_index

time: 238 us -> 221 us (0.929)
  blocking collectives: 135 us -> 108 us
  waiting for transfers between devices: 0.69 us -> 9.52 us
    all_gather x1 -> x0, blocking collectives: 20.1 us -> none  [shards(): lax.all_gather(unit_docs, 'dp', axis=0, tiled=True)]
    ppermute x0 -> x4, waiting for transfers between devices: none -> 8.83 us  [collect(): theirs = lax.ppermute(grown, axis, [(d, d ^ reach) for d in range(ways)])]
    unnamed x2, blocking collectives: 79.8 us -> 72.7 us
  transfers between devices with their start and end apart: 3 -> 7, of which waited for: 0 -> 3; matrix products, arithmetic and copies ran while one was open for 27% -> 29% of each run, Pallas kernels for 0% -> 0%
where the time goes in v1:
time: 221 us
  blocking collectives  108 us (49%)
  local copies, waits for them, and re-layouts  38.3 us (17%)
  matrix products  19.3 us (9%)
  other arithmetic  16.2 us (7%)
  between operations  14.9 us (7%)
  starting transfers between devices  14.4 us (7%)
  waiting for transfers between devices  9.52 us (4%)
    unnamed x2, blocking collectives  72.7 us
    psum x1, blocking collectives, shards(): totals = lax.psum(keep_flags.astype(jnp.float32), 'dp').astype(jnp.int32)  35.5 us
    dot_general x1, matrix products, project(): row_sum = jnp.dot(rows, piece, preferred_element_type=jnp.float32)  10.5 us
    scatter x1, local copies, waits for them, and re-layouts, send_to_owners(): jnp.zeros((row_count, width), rows.dtype).at[targets]  9.31 us
    ppermute x4, waiting for transfers between devices, collect(): theirs = lax.ppermute(grown, axis, [(d, d ^ reach) for d in range(ways)])  8.83 us
    convert_element_type x2, local copies, waits for them, and re-layouts, attend(): attended.reshape(doc_count, length, features).astype(jnp.bfloat16)  7.39 us
    scatter x1, other arithmetic, send_to_owners(): jnp.zeros((axis_size * capacity, width), rows.dtype).at[slots]  7.38 us
    all_to_all x1, starting transfers between devices, send_to_owners(): lax.all_to_all(packed_keys.reshape(axis_size, capacity), 'dp', split_axis...  6.32 us
  transfers between devices with their start and end apart: 7, of which 3 were waited for; matrix products, arithmetic and copies ran while one was open for 29% of the time, Pallas kernels for 0%

profile of v1, /device:TPU:0, one launch (start us, length us, event | category | flops | bytes accessed | tf_op | source)
XLA Modules:
  0.0 220.8 jit_solution(16109528788444276348)
XLA Ops:
  8.6 35.5 %psum.7 = f32[4]{0:T(128)S(1)} all-reduce(f32[4]{0:T(128)S(1)} %convert_element_type.46), channel_id=1, replica_groups=mesh['groups'=2,'dp'=16] {'dp'}, use_global_device_ids=true, to_apply=%region_0.1 | all-reduce | flops 4 | bytes 32 | tf_op jit(solution)/shard_map/psum | solution.py:124
  44.1 1.2 dynamic-slice
  46.0 0.9 dynamic-update-slice
  46.9 8.3 %all-reduce = s32[64]{0:T(128)S(1)} all-reduce(s32[64]{0:T(128)S(1)} %dynamic-update-slice), channel_id=2, replica_groups=mesh['groups'=2,'dp'=16] {'dp'}, use_global_device_ids=true, to_apply=%add | all-reduce | flops 64 | bytes 512
  55.4 0.7 fusion.40
  56.1 2.3 %gather_fusion = s32[512]{0:T(512)S(1)} fusion(s32[1024]{0:T(1024)S(1)} %copy-done, s32[1024]{0:T(1024)S(1)} %pad_clamp_fusion), kind=kCustom, calls=%fused_computation | custom fusion | bytes 6144 | tf_op jit(solution)/shard_map/jit(_take)/gather | solution.py:132
  59.8 0.8 select_bitcast_fusion
  60.5 0.7 bitcast_select_fusion.1
  61.2 1.2 reduce-window.20
  62.8 4.5 %gather_fusion.1 = s32[512]{0:T(512)S(1)} fusion(s32[512,16]{0,1:T(8,128)S(1)} %bitcast_bitcast_fusion, s32[512]{0:T(512)S(1)} %bitcast.76), kind=kCustom, calls=%fused_computation.1 | custom fusion | bytes 8192 | tf_op jit(solution)/shard_map/jit(take_along_axis)/gather | solution.py:88
  67.3 2.4 %scatter_custom_fusion = s32[768]{0:T(1024)S(1)} fusion(s32[512]{0:T(512)S(1)} %bitcast.86, s32[512]{0:T(512)S(1)} %get-tuple-element.35, s32[]{:T(128)} %constant.31.clone.1), kind=kCustom, calls=%fused_computation.76 | custom fusion | bytes 3076 | tf_op jit(solution)/shard_map/scatter | solution.py:92
  69.8 0.7 all_to_all.9
  70.5 6.3 %all-to-all-start = ((s32[16,1,48]{2,1,0:T(1,128)}), s32[16,1,48]{2,1,0:T(1,128)S(1)}, u32[]{:S(2)}, u32[]{:S(2)}) async-start(s32[16,1,48]{2,1,0:T(1,128)} %all_to_all.9), calls=%async_computation | async-start | bytes 16384 | tf_op jit(solution)/shard_map/all_to_all | solution.py:102
  76.8 1.0 copy.40
  77.8 3.3 %reshape.386 = bf16[4,128,4,4,128]{4,3,2,1,0:T(4,128)(2,1)S(1)} reshape(bf16[4,128,2048]{2,1,0:T(8,128)(2,1)} %param.10) | data formatting | bytes 4194304 | tf_op jit(solution)/shard_map/reshape | solution.py:48
  81.2 0.7 fusion.6
  82.0 1.7 fusion.51
  83.7 0.7 fusion.13
  84.4 2.9 %copy.32 = bf16[4,128,4,4,128]{4,3,2,1,0:T(4,128)(2,1)} copy(bf16[4,128,4,4,128]{1,4,3,2,0:T(8,128)(2,1)S(1)} %bitcast.77) | data formatting | bytes 4194304 | tf_op jit(solution)/shard_map/convert_element_type | solution.py:62
  87.3 4.5 %convert_element_type.57 = bf16[512,2048]{1,0:T(8,128)(2,1)} reshape(bf16[4,128,4,4,128]{4,3,2,1,0:T(4,128)(2,1)} %copy.32) | data formatting | bytes 4194304 | tf_op jit(solution)/shard_map/convert_element_type | solution.py:62
  91.8 10.5 %multiply_reduce_fusion = (f32[512]{0:T(512)S(1)}, f32[512,2048]{1,0:T(8,128)}) fusion(bf16[512,2048]{1,0:T(8,128)(2,1)} %convert_element_type.57, bf16[2048,2048]{1,0:T(8,128)(2,1)} %all-gather.3.cloned.1.call-done), kind=kOutput, calls=%fused_computation.13 | convolution fusion | flops 4297063936 | bytes 14682112 | tf_op jit(solution)/shard_map/dot_general | solution.py:75
  102.3 7.4 %scatter_custom_fusion.1 = bf16[768,2048]{1,0:T(8,128)(2,1)} fusion(s32[512]{0:T(512)S(1)} %bitcast.87, f32[512,2048]{1,0:T(8,128)} %get-tuple-element.45, f32[512]{0:T(512)S(1)} %add_rsqrt_fusion, bf16[]{:T(256)} %constant.43.clone.1), kind=kCustom, calls=%fused_computation.18 | custom fusion | flops 2097152 | bytes 7342082 | tf_op jit(solution)/shard_map/scatter | solution.py:90
  109.7 6.0 %all-to-all-start.1 = ((bf16[16,48,2048]{2,1,0:T(8,128)(2,1)}), bf16[16,48,2048]{2,1,0:T(8,128)(2,1)}, u32[]{:S(2)}, u32[]{:S(2)}) async-start(bf16[16,48,2048]{2,1,0:T(8,128)(2,1)} %bitcast.23), calls=%async_computation.1 | async-start | bytes 6291456 | tf_op jit(solution)/shard_map/all_to_all | solution.py:95
  116.4 5.9 %multiply_reduce_fusion.1 = (f32[4]{0:T(128)S(1)}, f32[4,2048]{1,0:T(4,128)S(1)}) fusion(bf16[2048,2048]{1,0:T(8,128)(2,1)} %all-gather.3.cloned.1.call-done, f32[4,1,2048]{2,1,0:T(1,128)S(1)} %fusion.31, f32[4]{0:T(128)S(1)} %convert_reduce_fusion.1), kind=kOutput, calls=%fused_computation.50 | convolution fusion | flops 201351168 | bytes 8454176 | tf_op jit(solution)/shard_map/dot_general | solution.py:76
  123.0 64.4 %all-reduce.1 = s32[64]{0:T(128)S(1)} all-reduce(s32[64]{0:T(128)S(1)} %dynamic-update-slice.1), channel_id=1, replica_groups=mesh['groups'=2,'dp'=16] {'dp'}, use_global_device_ids=true, to_apply=%add.1 | all-reduce | flops 64 | bytes 512
  188.7 1.5 collective-permute-start.1
  190.3 2.4 %collective-permute-done.1 = bf16[8,2048]{1,0:T(8,128)(2,1)S(1)} collective-permute-done((bf16[8,2048]{1,0:T(8,128)(2,1)S(1)}, bf16[8,2048]{1,0:T(8,128)(2,1)S(1)}, u32[]{:S(2)}, u32[]{:S(2)}) %collective-permute-start.1) | collective-permute-done | bytes 32800 | tf_op jit(solution)/shard_map/ppermute | solution.py:14
  193.3 3.8 %collective-permute-done.2 = bf16[16,2048]{1,0:T(8,128)(2,1)S(1)} collective-permute-done((bf16[16,2048]{1,0:T(8,128)(2,1)S(1)}, bf16[16,2048]{1,0:T(8,128)(2,1)S(1)}, u32[]{:S(2)}, u32[]{:S(2)}) %collective-permute-start.2) | collective-permute-done | bytes 65568 | tf_op jit(solution)/shard_map/ppermute | solution.py:14
  197.3 3.9 %scatter_custom_fusion.3 = s32[512]{0:T(512)} fusion(s32[768]{0:T(1024)S(1)} %fusion.33, s32[768]{0:T(1024)S(1)} %reshape.438, s32[]{:T(128)} %constant.31.clone.1), kind=kCustom, calls=%fused_computation.81 | custom fusion | bytes 2052 | tf_op jit(solution)/shard_map/scatter | solution.py:112
  201.2 2.6 %collective-permute-done.3 = bf16[32,2048]{1,0:T(8,128)(2,1)S(1)} collective-permute-done((bf16[32,2048]{1,0:T(8,128)(2,1)S(1)}, bf16[32,2048]{1,0:T(8,128)(2,1)S(1)}, u32[]{:S(2)}, u32[]{:S(2)}) %collective-permute-start.3) | collective-permute-done | bytes 131104 | tf_op jit(solution)/shard_map/ppermute | solution.py:14
  203.8 0.8 convolution_convert_fusion
  204.7 9.3 %scatter_custom_fusion.2 = bf16[512,2048]{1,0:T(8,128)(2,1)} fusion(s32[768]{0:T(1024)S(1)} %fusion.33, bf16[768,2048]{1,0:T(8,128)(2,1)} %bitcast.24, bf16[]{:T(256)} %constant.43.clone.1), kind=kCustom, calls=%fused_computation.28 | custom fusion | bytes 2097664 | tf_op jit(solution)/shard_map/scatter | solution.py:111
  (57 shorter events, 7.1 us)
Async XLA Ops:
  7.2 49.0 %copy-start = (s32[1024]{0:T(1024)S(1)}, s32[1024]{0:T(1024)}, u32[]{:S(2)}) copy-start(s32[1024]{0:T(1024)} %param.17) | copy-start | bytes 12292
  7.2 69.6 %copy-start.1 = (bf16[4,128,512]{2,1,0:T(8,128)(2,1)S(1)}, bf16[4,128,512]{2,1,0:T(8,128)(2,1)}, u32[]{:S(2)}) copy-start(bf16[4,128,512]{2,1,0:T(8,128)(2,1)} %param.12) | copy-start | bytes 1572868
  7.2 84.6 %all-gather.3.cloned.1.call-start = ((), (), s32[]{:S(2)}) async-start(), calls=%async_computation.2 | async-start | bytes 8912896 | tf_op jit(solution)/shard_map/all_gather | solution.py:74
  67.3 13.8 %copy-start.2 = (bf16[4,128,512]{2,1,0:T(8,128)(2,1)S(1)}, bf16[4,128,512]{2,1,0:T(8,128)(2,1)}, u32[]{:S(2)}) copy-start(bf16[4,128,512]{2,1,0:T(8,128)(2,1)} %param.11) | copy-start | bytes 1572868
  70.5 39.2 %all-to-all-start = ((s32[16,1,48]{2,1,0:T(1,128)}), s32[16,1,48]{2,1,0:T(1,128)S(1)}, u32[]{:S(2)}, u32[]{:S(2)}) async-start(s32[16,1,48]{2,1,0:T(1,128)} %all_to_all.9), calls=%async_computation | async-start | bytes 16384 | tf_op jit(solution)/shard_map/all_to_all | solution.py:102
  82.0 1.7 copy-start.3
  109.7 95.0 %all-to-all-start.1 = ((bf16[16,48,2048]{2,1,0:T(8,128)(2,1)}), bf16[16,48,2048]{2,1,0:T(8,128)(2,1)}, u32[]{:S(2)}, u32[]{:S(2)}) async-start(bf16[16,48,2048]{2,1,0:T(8,128)(2,1)} %bitcast.23), calls=%async_computation.1 | async-start | bytes 6291456 | tf_op jit(solution)/shard_map/all_to_all | solution.py:95
  122.4 66.2 %collective-permute-start = (bf16[4,2048]{1,0:T(4,128)(2,1)S(1)}, bf16[4,2048]{1,0:T(4,128)(2,1)S(1)}, u32[]{:S(2)}, u32[]{:S(2)}) collective-permute-start(bf16[4,2048]{1,0:T(4,128)(2,1)S(1)} %multiply_convert_fusion.2), channel_id=1, source_target_pairs={{0,1},{1,0},{2,3},{3,2},{4,5},{5,4},{6,7},{7,6},{8,9},{9,8},{10,11... | collective-permute-start | bytes 49160 | tf_op jit(solution)/shard_map/ppermute | solution.py:14
  188.7 4.0 %collective-permute-start.1 = (bf16[8,2048]{1,0:T(8,128)(2,1)S(1)}, bf16[8,2048]{1,0:T(8,128)(2,1)S(1)}, u32[]{:S(2)}, u32[]{:S(2)}) collective-permute-start(bf16[8,2048]{1,0:T(8,128)(2,1)S(1)} %maximum_select_fusion.4), channel_id=1, source_target_pairs={{0,2},{1,3},{2,0},{3,1},{4,6},{5,7},{6,4},{7,5},{8,10},{9,11},{10,... | collective-permute-start | bytes 98312 | tf_op jit(solution)/shard_map/ppermute | solution.py:14
  192.7 4.3 %collective-permute-start.2 = (bf16[16,2048]{1,0:T(8,128)(2,1)S(1)}, bf16[16,2048]{1,0:T(8,128)(2,1)S(1)}, u32[]{:S(2)}, u32[]{:S(2)}) collective-permute-start(bf16[16,2048]{1,0:T(8,128)(2,1)S(1)} %maximum_select_fusion.3), channel_id=1, source_target_pairs={{0,4},{1,5},{2,6},{3,7},{4,0},{5,1},{6,2},{7,3},{8,12},{9,13},{10,... | collective-permute-start | bytes 196616 | tf_op jit(solution)/shard_map/ppermute | solution.py:14
  197.1 6.8 %collective-permute-start.3 = (bf16[32,2048]{1,0:T(8,128)(2,1)S(1)}, bf16[32,2048]{1,0:T(8,128)(2,1)S(1)}, u32[]{:S(2)}, u32[]{:S(2)}) collective-permute-start(bf16[32,2048]{1,0:T(8,128)(2,1)S(1)} %maximum_select_fusion.2), channel_id=1, source_target_pairs={{0,8},{1,9},{2,10},{3,11},{4,12},{5,13},{6,14},{7,15},{8,0},{9,1},... | collective-permute-start | bytes 393224 | tf_op jit(solution)/shard_map/ppermute | solution.py:14
Sparse Core Ops, SparseCore 0:
  10.2 78.0 all-gather.2
